TPU v7x, 512 devices: a whole 4x4x16 slice. The times are simulated.
512 devices in a mesh: box: 64 (over y, z_lo, core), samp: 8 (over x, z_hi).
Axes of the slice: x: 4, y: 4, z: 16 (z_hi: 2, z_lo: 8; z = z_hi * 8 + z_lo), core: 2. Of those that a mesh axis runs over, the one named last changes fastest.
Arguments:
- currents: bfloat16 [16, 2, 32768], P(None, None, 'box'), may hold values from -6 to 6
- radiation: bfloat16 [2, 512, 64, 2048], P(None, 'box', None, 'samp'), may hold values from -0.5 to 0.5
- interp: bfloat16 [2, 3, 2, 2048, 256], P(None, None, None, 'samp'), may hold values from -0.1875 to 0.1875
- translation: bfloat16 [2, 316, 2048], P(None, None, 'samp'), may hold values from -1 to 1
- inter_owner: int32 [512, 4], P('box'), may hold values from 0 to 63, all different within a row; in each aligned block of 8 rows (0 to 7, 8 to 15, ...) at most 2 rows name the same one
- inter_local: int32 [512, 4, 2], P('box'), may hold values from 0 to 7
- inter_type: int32 [512, 4, 2], P('box'), may hold values from 0 to 315
- near_blocks: bfloat16 [2, 16384, 64, 64], P(None, ('box', 'samp')), may hold values from -0.09375 to 0.09375
- near_index: int32 [16384, 2], P(('box', 'samp')), may hold values from 0 to 511, as said below
Outputs:
- field: float32 [16, 2, 32768], P('samp', None, 'box')
Inputs may be any that keep to these rules, and one draw needn't show every extreme that they name: `inter_owner`: each box names 4 different owners; among the 8 boxes of one box index no owner is named more than 2 times. `near_index`: the blocks of one device receive on boxes of that device's box index; each source box is one of those boxes or of the 8 boxes on either side.
All inputs are finite; a program needn't handle non-finite values.
Results may differ from a plain program's by a relative error of at most 0.0075.
Values may be sent and summed in bfloat16 or wider, within the bound.
A program may use at most 64 MiB of HBM per device.

v0:
```python
import math

import jax
import jax.numpy as jnp
from jax import lax
from jax.sharding import PartitionSpec as P

M = 64
K = 2048
OWN = 4
PER = 2


def swapped(block, axis, distance):
    count = lax.axis_size(axis)
    route = []
    for low in range(count):
        high = low | 1 << distance
        if high != low and high < count:
            route += [(low, high), (high, low)]
    return lax.ppermute(block, axis, route)


def with_halo(cells, sides, width):
    for axis, dim in sides:
        count = lax.axis_size(axis)
        ends = count - 1
        head = lax.slice_in_dim(cells, 0, width, axis=dim)
        tail = lax.slice_in_dim(cells, cells.shape[dim] - width, cells.shape[dim], axis=dim)
        cells = jnp.concatenate(
            [
                lax.ppermute(tail, axis, [(i, (i + 1) % count) for i in range(ends)]),
                cells,
                lax.ppermute(head, axis, [((i + 1) % count, i) for i in range(ends)]),
            ],
            axis=dim,
        )
    return cells


def mat_rows(left, right):
    return jnp.dot(left, right, preferred_element_type=jnp.float32)


def local(
    currents,
    radiation,
    interp,
    translation,
    inter_owner,
    inter_local,
    inter_type,
    near_blocks,
    near_index,
):
    rhs_count = currents.shape[0]
    box_dev = inter_owner.shape[0]
    owner_count = inter_owner.shape[1]
    entry_count = inter_local.shape[2]
    unknowns = radiation.shape[2]
    sample_count = radiation.shape[3]
    box_count = lax.axis_size("box")
    samp_count = lax.axis_size("samp")
    current_grid = currents.reshape(rhs_count, 2, box_dev, unknowns)
    agg_real = jnp.einsum(
        "bmk,rbm->brk", radiation[0], current_grid[:, 0], preferred_element_type=jnp.float32
    ) - jnp.einsum(
        "bmk,rbm->brk", radiation[1], current_grid[:, 1], preferred_element_type=jnp.float32
    )
    agg_imag = jnp.einsum(
        "bmk,rbm->brk", radiation[0], current_grid[:, 1], preferred_element_type=jnp.float32
    ) + jnp.einsum(
        "bmk,rbm->brk", radiation[1], current_grid[:, 0], preferred_element_type=jnp.float32
    )
    pattern = jnp.stack([agg_real, agg_imag], axis=1).astype(jnp.bfloat16)
    level_count = samp_count.bit_length() - 1
    flat_rows = box_dev * rhs_count
    for bit_level in range(level_count):
        partner = swapped(pattern, "samp", bit_level)
        weights = interp[:, bit_level]
        own_real = pattern[:, 0].reshape(flat_rows, sample_count)
        own_imag = pattern[:, 1].reshape(flat_rows, sample_count)
        pair_real = partner[:, 0].reshape(flat_rows, sample_count)
        pair_imag = partner[:, 1].reshape(flat_rows, sample_count)
        new_real = (
            mat_rows(own_real, weights[0, 0])
            - mat_rows(own_imag, weights[1, 0])
            + mat_rows(pair_real, weights[0, 1])
            - mat_rows(pair_imag, weights[1, 1])
        )
        new_imag = (
            mat_rows(own_real, weights[1, 0])
            + mat_rows(own_imag, weights[0, 0])
            + mat_rows(pair_real, weights[1, 1])
            + mat_rows(pair_imag, weights[0, 1])
        )
        pattern = jnp.stack(
            [
                new_real.reshape(box_dev, rhs_count, sample_count),
                new_imag.reshape(box_dev, rhs_count, sample_count),
            ],
            axis=1,
        ).astype(jnp.bfloat16)
    capacity = max(2, box_dev * owner_count // box_count)
    owner_hits = jnp.sum(
        (inter_owner[:, :, None] == jnp.arange(box_count, dtype=jnp.int32)).astype(jnp.int32),
        axis=1,
    )
    earlier = jnp.cumsum(owner_hits, axis=0) - owner_hits
    slot_rank = jnp.take_along_axis(earlier, inter_owner, axis=1)
    dest_table = (
        jnp.full((box_count, capacity, entry_count), box_dev, jnp.int32)
        .at[inter_owner, slot_rank]
        .set(inter_local)
    )
    box_labels = jnp.arange(box_dev, dtype=jnp.int32)
    chosen = translation[:, inter_type]
    chosen_real = chosen[0][:, :, :, None, :].astype(jnp.float32)
    chosen_imag = chosen[1][:, :, :, None, :].astype(jnp.float32)
    source_real = pattern[:, 0][:, None, None].astype(jnp.float32)
    source_imag = pattern[:, 1][:, None, None].astype(jnp.float32)
    part_real = chosen_real * source_real - chosen_imag * source_imag
    part_imag = chosen_real * source_imag + chosen_imag * source_real
    partials = jnp.stack([part_real, part_imag], axis=3).astype(jnp.bfloat16)
    outgoing = (
        jnp.zeros((box_count, capacity, entry_count, 2, rhs_count, sample_count), jnp.bfloat16)
        .at[inter_owner, slot_rank]
        .set(partials)
    )
    arrived, arrived_dest = (
        lax.all_to_all(outgoing, "box", split_axis=0, concat_axis=0, tiled=True),
        lax.all_to_all(dest_table, "box", split_axis=0, concat_axis=0, tiled=True),
    )
    target_hot = (arrived_dest[..., None] == box_labels).astype(jnp.bfloat16)
    incoming = jnp.einsum(
        "scpd,scpxrk->xdrk", target_hot, arrived, preferred_element_type=jnp.float32
    )
    incoming_rounded = incoming.astype(jnp.bfloat16)
    far_scale = math.sqrt(M / (K * OWN * PER))
    far_real = jnp.einsum(
        "bmk,brk->rbm", radiation[0], incoming_rounded[0], preferred_element_type=jnp.float32
    ) + jnp.einsum(
        "bmk,brk->rbm", radiation[1], incoming_rounded[1], preferred_element_type=jnp.float32
    )
    far_imag = jnp.einsum(
        "bmk,brk->rbm", radiation[0], incoming_rounded[1], preferred_element_type=jnp.float32
    ) - jnp.einsum(
        "bmk,brk->rbm", radiation[1], incoming_rounded[0], preferred_element_type=jnp.float32
    )
    far_part = far_scale * jnp.stack([far_real, far_imag], axis=1)
    neighbours = with_halo(currents, (("box", 2),), box_dev * unknowns)
    near_grid = neighbours.reshape(rhs_count, 2, 3 * box_dev, unknowns)
    first_box = (lax.axis_index("box") - 1) * box_dev
    source_slot = near_index[:, 1] - first_box
    target_slot = near_index[:, 0] - first_box - box_dev
    picked = near_grid[:, :, source_slot, :]
    near_real = jnp.einsum(
        "nij,rnj->rni", near_blocks[0], picked[:, 0], preferred_element_type=jnp.float32
    ) - jnp.einsum("nij,rnj->rni", near_blocks[1], picked[:, 1], preferred_element_type=jnp.float32)
    near_imag = jnp.einsum(
        "nij,rnj->rni", near_blocks[0], picked[:, 1], preferred_element_type=jnp.float32
    ) + jnp.einsum("nij,rnj->rni", near_blocks[1], picked[:, 0], preferred_element_type=jnp.float32)
    contrib = jnp.stack([near_real, near_imag], axis=1)
    near_hot = (target_slot[:, None] == box_labels).astype(jnp.float32)
    near_part = jnp.einsum("rcnm,nd->rcdm", contrib, near_hot, precision=lax.Precision.HIGHEST)
    total = (near_part + far_part).reshape(rhs_count, 2, box_dev * unknowns)
    return lax.psum_scatter(total, "samp", scatter_dimension=0, tiled=True)


def solution(mesh):
    in_specs = (
        P(None, None, "box"),
        P(None, "box", None, "samp"),
        P(None, None, None, "samp", None),
        P(None, None, "samp"),
        P("box", None),
        P("box", None, None),
        P("box", None, None),
        P(None, ("box", "samp"), None, None),
        P(("box", "samp"), None),
    )
    out_specs = P("samp", None, "box")
    return jax.shard_map(local, mesh=mesh, in_specs=in_specs, out_specs=out_specs, check_vma=False)
```

profile of v0, /device:TPU:6, one launch (start us, length us, event | category | flops | bytes accessed | tf_op | source)
XLA Modules:
  0.0 447.5 jit_solution(16202868324444863057)
XLA Ops:
  6.5 1.0 reshape.132
  7.6 1.1 fusion.51
  8.7 1.1 fusion.49
  9.8 1.1 fusion.20
  10.9 1.1 fusion.21
  12.7 15.7 %collective-permute-start.2 = (bf16[8,2,16,256]{3,2,0,1:T(8,128)(2,1)}, bf16[8,2,16,256]{3,2,0,1:T(8,128)(2,1)}, u32[]{:S(2)}, u32[]{:S(2)}) collective-permute-start(bf16[8,2,16,256]{3,2,0,1:T(8,128)(2,1)} %pad_maximum_fusion.2), channel_id=1, source_target_pairs={{0,1},{1,0},{2,3},{3,2},{4,5},{5,4},{6,7},{7,6},{8,9},{9,8},{10,11... | collective-permute-start | bytes 393224 | tf_op jit(solution)/shard_map/ppermute | solution.py:21
  28.4 0.8 copy.120
  29.2 0.8 convert_reduce_fusion
  32.1 3.7 scatter_fusion.1
  35.7 9.0 %all-to-all-start.1 = ((s32[64,2,2]{2,1,0:T(2,128)}), s32[64,2,2]{2,1,0:T(2,128)}, u32[]{:S(2)}, u32[]{:S(2)}) async-start(s32[64,2,2]{2,1,0:T(2,128)} %scatter_fusion.1), calls=%async_computation.1 | async-start | bytes 131072 | tf_op jit(solution)/shard_map/all_to_all | solution.py:132
  44.8 1.0 fusion.61
  45.8 1.0 fusion.62
  47.4 0.7 gather_fusion.1
  48.3 0.9 fusion.92
  50.4 2.7 collective-permute-start.3
  53.3 4.4 collective-permute-done.3
  58.9 3.5 collective-permute-start.4
  62.6 4.7 %collective-permute-done.4 = bf16[8,2,16,256]{3,2,0,1:T(8,128)(2,1)S(1)} collective-permute-done((bf16[8,2,16,256]{3,2,0,1:T(8,128)(2,1)S(1)}, bf16[8,2,16,256]{3,2,0,1:T(8,128)(2,1)S(1)}, u32[]{:S(2)}, u32[]{:S(2)}) %collective-permute-start.4) | collective-permute-done | bytes 131104 | tf_op jit(solution)/shard_map/ppermute | solution.py:21
  68.5 2.5 broadcast_in_dim.12
  71.0 5.0 %scatter_fusion = bf16[64,2,2,2,16,256]{5,4,3,2,1,0:T(8,128)(2,1)} fusion(bf16[64,2,2,2,16,256]{5,4,3,2,1,0:T(8,128)(2,1)} %broadcast_in_dim.12, s32[32]{0:T(128)S(1)} %reshape.113, bf16[32,2,2,16,256]{4,3,2,1,0:T(8,128)(2,1)S(1)} %bitcast.220), kind=kCustom, calls=%fused_computation.3 | custom fusion | bytes 3145984 | tf_op jit(solution)/shard_map/scatter | solution.py:128
  76.0 11.9 %copy.131 = bf16[64,2,2,2,16,256]{5,2,1,4,3,0:T(2,128)(2,1)} copy(bf16[64,2,2,2,16,256]{5,4,3,2,1,0:T(8,128)(2,1)} %scatter_fusion) | data formatting | bytes 8388608 | tf_op jit(solution)/shard_map/scatter | solution.py:128
  87.9 13.5 %all-to-all-start = ((bf16[64,2,2,2,16,256]{5,2,1,4,3,0:T(2,128)(2,1)}), bf16[64,2,2,2,16,256]{5,2,1,4,3,0:T(2,128)(2,1)}, u32[]{:S(2)}, u32[]{:S(2)}) async-start(bf16[64,2,2,2,16,256]{5,2,1,4,3,0:T(2,128)(2,1)} %copy.131), calls=%async_computation | async-start | bytes 8388608 | tf_op jit(solution)/shard_map/all_to_all | solution.py:131
  101.5 1.9 collective-permute-start
  103.4 1.5 collective-permute-start.1
  105.0 0.9 copy.134
  105.9 1.8 collective-permute-done.1
  110.2 173.8 %all-to-all-done = bf16[64,2,2,2,16,256]{5,2,1,4,3,0:T(2,128)(2,1)} async-done(((bf16[64,2,2,2,16,256]{5,2,1,4,3,0:T(2,128)(2,1)}), bf16[64,2,2,2,16,256]{5,2,1,4,3,0:T(2,128)(2,1)}, u32[]{:S(2)}, u32[]{:S(2)}) %all-to-all-start) | async-done | bytes 4194336 | tf_op jit(solution)/shard_map/all_to_all | solution.py:131
  284.1 6.6 %fusion.16 = bf16[2,8,16,256]{3,1,2,0:T(8,128)(2,1)S(1)} fusion(bf16[64,2,2,2,16,256]{5,2,1,4,3,0:T(2,128)(2,1)} %all-to-all-done, s32[64,2,2]{0,2,1:T(2,128)S(1)} %copy.134), kind=kOutput, calls=%fused_computation.31 | convolution fusion | flops 33622016 | bytes 4326400 | tf_op jit(solution)/shard_map/scpd,scpxrk->xdrk/dot_general | solution.py:135
  292.0 0.7 reshape.86
  292.7 1.3 dynamic-slice
  294.7 144.7 %all-reduce.3.cloned.1.call-done = f32[16,2,512]{2,1,0:T(2,128)} async-done(((f32[16,2,512]{2,1,0:T(2,128)}), f32[16,2,512]{2,1,0:T(2,128)}) %all-reduce.3.cloned.1.call-update) | async-done | bytes 65552
  439.3 1.3 constant_dynamic-slice_fusion
  (98 shorter events, 11.3 us)
Async XLA Ops:
  6.5 40.9 %copy-start = (bf16[2,316,256]{2,0,1:T(2,128)(2,1)S(1)}, bf16[2,316,256]{2,0,1:T(2,128)(2,1)}, u32[]{:S(2)}) copy-start(bf16[2,316,256]{2,0,1:T(2,128)(2,1)} %param.12) | copy-start | bytes 970756
  6.5 24.8 %copy-start.6 = (s32[8,4,2]{0,2,1:T(2,128)S(1)}, s32[8,4,2]{0,2,1:T(2,128)}, u32[]{:S(2)}) copy-start(s32[8,4,2]{0,2,1:T(2,128)} %param.14) | copy-start | bytes 772
  6.5 38.1 %copy-start.3 = (bf16[2,3,2,256,256]{4,3,2,1,0:T(8,128)(2,1)S(1)}, bf16[2,3,2,256,256]{4,3,2,1,0:T(8,128)(2,1)}, u32[]{:S(2)}) copy-start(bf16[2,3,2,256,256]{4,3,2,1,0:T(8,128)(2,1)} %param.11) | copy-start | bytes 4718596
  10.9 1.1 copy-start.4
  12.7 35.6 %collective-permute-start.2 = (bf16[8,2,16,256]{3,2,0,1:T(8,128)(2,1)}, bf16[8,2,16,256]{3,2,0,1:T(8,128)(2,1)}, u32[]{:S(2)}, u32[]{:S(2)}) collective-permute-start(bf16[8,2,16,256]{3,2,0,1:T(8,128)(2,1)} %pad_maximum_fusion.2), channel_id=1, source_target_pairs={{0,1},{1,0},{2,3},{3,2},{4,5},{5,4},{6,7},{7,6},{8,9},{9,8},{10,11... | collective-permute-start | bytes 393224 | tf_op jit(solution)/shard_map/ppermute | solution.py:21
  30.3 16.9 %copy-start.7 = (s32[8,4,2]{0,2,1:T(2,128)S(1)}, s32[8,4,2]{0,2,1:T(2,128)}, u32[]{:S(2)}) copy-start(s32[8,4,2]{0,2,1:T(2,128)} %param.15) | copy-start | bytes 772
  35.7 52.2 %all-to-all-start.1 = ((s32[64,2,2]{2,1,0:T(2,128)}), s32[64,2,2]{2,1,0:T(2,128)}, u32[]{:S(2)}, u32[]{:S(2)}) async-start(s32[64,2,2]{2,1,0:T(2,128)} %scatter_fusion.1), calls=%async_computation.1 | async-start | bytes 131072 | tf_op jit(solution)/shard_map/all_to_all | solution.py:132
  50.4 7.3 %collective-permute-start.3 = (bf16[8,2,16,256]{3,2,0,1:T(8,128)(2,1)S(1)}, bf16[8,2,16,256]{3,2,0,1:T(8,128)(2,1)S(1)}, u32[]{:S(2)}, u32[]{:S(2)}) collective-permute-start(bf16[8,2,16,256]{3,2,0,1:T(8,128)(2,1)S(1)} %pad_maximum_fusion.3), channel_id=1, source_target_pairs={{0,2},{2,0},{1,3},{3,1},{4,6},{6,4},{5,7},{7,5},{8,10},{10,8},{9,1... | collective-permute-start | bytes 393224 | tf_op jit(solution)/shard_map/ppermute | solution.py:21
  58.9 8.4 %collective-permute-start.4 = (bf16[8,2,16,256]{3,2,0,1:T(8,128)(2,1)S(1)}, bf16[8,2,16,256]{3,2,0,1:T(8,128)(2,1)S(1)}, u32[]{:S(2)}, u32[]{:S(2)}) collective-permute-start(bf16[8,2,16,256]{3,2,0,1:T(8,128)(2,1)S(1)} %pad_maximum_fusion.4), channel_id=1, source_target_pairs={{0,4},{4,0},{1,5},{5,1},{2,6},{6,2},{3,7},{7,3},{8,12},{12,8},{9,1... | collective-permute-start | bytes 393224 | tf_op jit(solution)/shard_map/ppermute | solution.py:21
  87.9 13.6 %copy-start.5 = (bf16[16,2,512]{2,1,0:T(2,128)(2,1)S(1)}, bf16[16,2,512]{2,1,0:T(2,128)(2,1)}, u32[]{:S(2)}) copy-start(bf16[16,2,512]{2,1,0:T(2,128)(2,1)} %param.9) | copy-start | bytes 98308
  87.9 17.0 %copy-start.8 = (s32[32,2]{0,1:T(2,128)S(1)}, s32[32,2]{0,1:T(2,128)}, u32[]{:S(2)}) copy-start(s32[32,2]{0,1:T(2,128)} %param.17) | copy-start | bytes 772
  87.9 20.7 %copy-start.2 = (bf16[2,32,64,64]{3,2,1,0:T(8,128)(2,1)S(1)}, bf16[2,32,64,64]{3,2,1,0:T(8,128)(2,1)}, u32[]{:S(2)}) copy-start(bf16[2,32,64,64]{3,2,1,0:T(8,128)(2,1)} %param.16) | copy-start | bytes 1572868
  87.9 196.1 %all-to-all-start = ((bf16[64,2,2,2,16,256]{5,2,1,4,3,0:T(2,128)(2,1)}), bf16[64,2,2,2,16,256]{5,2,1,4,3,0:T(2,128)(2,1)}, u32[]{:S(2)}, u32[]{:S(2)}) async-start(bf16[64,2,2,2,16,256]{5,2,1,4,3,0:T(2,128)(2,1)} %copy.131), calls=%async_computation | async-start | bytes 8388608 | tf_op jit(solution)/shard_map/all_to_all | solution.py:131
  101.5 337.9 %all-reduce.3.cloned.1.call-start = ((), (), s32[]{:S(2)}) async-start(), calls=%async_computation.2 | async-start | bytes 131072
  101.5 4.4 collective-permute-start
  103.4 4.2 collective-permute-start.1
  109.4 181.3 %copy-start.1 = (bf16[2,8,64,256]{3,2,1,0:T(8,128)(2,1)S(1)}, bf16[2,8,64,256]{3,2,1,0:T(8,128)(2,1)}, u32[]{:S(2)}) copy-start(bf16[2,8,64,256]{3,2,1,0:T(8,128)(2,1)} %param.10) | copy-start | bytes 1572868
Sparse Core Ops, SparseCore 0:
  292.9 146.4 all-reduce.2
where the time goes:
time: 450 us; the launch traced here: 447 us
  waiting for transfers between devices  329 us (73%)
  starting transfers between devices  47.9 us (11%)
  local copies, waits for them, and re-layouts  34 us (8%)
  matrix products  19.3 us (4%)
  between operations  14.6 us (3%)
    all_to_all x1, waiting for transfers between devices, local(): lax.all_to_all(outgoing, 'box', split_axis=0, concat_axis=0, tiled=True)  174 us
    unnamed x2, waiting for transfers between devices  145 us
    ppermute x3, starting transfers between devices, swapped(): return lax.ppermute(block, axis, route)  21.9 us
    scatter x2, local copies, waits for them, and re-layouts, local(): outgoing = jnp.zeros((box_count, capacity, entry_count, 2, rhs_count, sam...  16.9 us
    all_to_all x1, starting transfers between devices, local(): lax.all_to_all(outgoing, 'box', split_axis=0, concat_axis=0, tiled=True)  13.5 us
    ppermute x3, waiting for transfers between devices, swapped(): return lax.ppermute(block, axis, route)  9.07 us
  transfers between devices with their start and end apart: 8, of which 5 were waited for; matrix products, arithmetic and copies ran while one was open for 9% of the time, Pallas kernels for 0%

commit v1 on v0

v1 whole, which is shorter than its diff:
```python
import functools
import math

import jax
import jax.numpy as jnp
from jax import lax
from jax.experimental import pallas as pl
from jax.experimental.pallas import tpu as pltpu
from jax.sharding import PartitionSpec as P

M = 64
K = 2048
OWN = 4
PER = 2
TYPES = 316
R = 16
B = 8
S = 256
NEAR = 32
NY, NZ, NC = 4, 8, 2
NS = 8
H = 2
RH = R // H
ROWS = R * 2 * B
HROWS = ROWS // H
LINE = NZ * NC
F32 = jnp.float32
BF16 = jnp.bfloat16
FAR_SCALE = math.sqrt(M / (K * OWN * PER))


def remote(src, dst, send, recv, device):
    return pltpu.make_async_remote_copy(
        src_ref=src,
        dst_ref=dst,
        send_sem=send,
        recv_sem=recv,
        device_id=device,
        device_id_type=pl.DeviceIdType.MESH,
    )


def dot(a, b):
    return jnp.dot(a, b, preferred_element_type=F32)


def dot_nt(a, b):
    return lax.dot_general(a, b, (((1,), (1,)), ((), ())), preferred_element_type=F32)


def kernel(
    cur_h,
    rad_h,
    itp_h,
    trn_h,
    near_h,
    owner_s,
    local_s,
    type_s,
    nidx_s,
    out_ref,
    cur,
    halo,
    rad,
    itp,
    trn,
    nb,
    cur32,
    expanded,
    grid,
    near_y,
    near2d,
    xb,
    yb,
    xg,
    tb,
    tr,
    ops,
    pb,
    hm,
    sb,
    sf,
    yr,
    fs,
    fr,
    in_sem,
    halo_ss,
    halo_rs,
    lev_ss,
    lev_rs,
    tab_ss,
    tab_rs,
    right_ss,
    right_rs,
    left_ss,
    left_rs,
    sib_ss,
    sib_rs,
    y_ss,
    y_rs,
    fin_ss,
    fin_rs,
):
    box = lax.axis_index("box")
    samp = lax.axis_index("samp")
    y = box // LINE
    g = box % LINE
    zl = g // NC
    c = g % NC
    line0 = y * LINE
    sibling = line0 + zl * NC + 1 - c
    zr_dev = (line0 + jnp.minimum(zl + 1, NZ - 1) * NC + c, samp)
    zl_dev = (line0 + jnp.maximum(zl - 1, 0) * NC + c, samp)
    sib_dev = (sibling, samp)
    has_prev = box > 0
    has_next = box < NY * LINE - 1
    prev_dev = (jnp.maximum(box - 1, 0), samp)
    next_dev = (jnp.minimum(box + 1, NY * LINE - 1), samp)
    prev_far = jnp.logical_and(has_prev, g == 0)
    next_far = jnp.logical_and(has_next, g == LINE - 1)

    barrier = pltpu.get_barrier_semaphore()

    def greet(device):
        pl.semaphore_signal(barrier, inc=1, device_id=device, device_id_type=pl.DeviceIdType.MESH)

    for k in range(1, NS):
        greet((box, (samp + k) % NS))
    for k in range(1, LINE):
        greet((line0 + (g + k) % LINE, samp))
    for k in range(1, NY):
        greet(((box + k * LINE) % (NY * LINE), samp))

    @pl.when(prev_far)
    def _():
        greet(prev_dev)

    @pl.when(next_far)
    def _():
        greet(next_dev)

    loads = [
        pltpu.make_async_copy(cur_h, cur, in_sem.at[0]),
        pltpu.make_async_copy(rad_h, rad, in_sem.at[1]),
        pltpu.make_async_copy(itp_h, itp, in_sem.at[2]),
        pltpu.make_async_copy(near_h, nb, in_sem.at[3]),
        pltpu.make_async_copy(trn_h, trn, in_sem.at[4]),
    ]
    for load in loads:
        load.start()

    row = lax.broadcasted_iota(jnp.int32, (128, 128), 0)
    lane8 = lax.broadcasted_iota(jnp.int32, (8, 128), 1)
    row_slot = row % 2
    row_owner = ((row // 2 % NY) * NZ + row // 16) * NC + row // 8 % NC

    def add_box(b, carry):
        value, count = carry
        for j in range(OWN):
            field = jnp.where(
                lane8 == 0,
                b,
                jnp.where(
                    lane8 == 1,
                    type_s[j * PER, b],
                    jnp.where(
                        lane8 == 2,
                        type_s[j * PER + 1, b],
                        jnp.where(
                            lane8 == 3,
                            local_s[j * PER, b],
                            jnp.where(lane8 == 4, local_s[j * PER + 1, b], -1),
                        ),
                    ),
                ),
            )
            hit = row_owner == owner_s[j, b]
            take = jnp.logical_and(hit, count == row_slot)
            wide = jnp.broadcast_to(field[None], (16, 8, 128)).reshape(128, 128)
            value = jnp.where(take, wide, value)
            count = count + jnp.where(hit, 1, 0)
        return value, count

    table, _ = lax.fori_loop(
        0, B, add_box, (jnp.full((128, 128), -1, jnp.int32), jnp.zeros((128, 128), jnp.int32))
    )
    tb[...] = table.reshape(LINE, 8, 128)

    lane_box = lax.broadcasted_iota(jnp.int32, (8, B * M), 1) // M
    own_box = lane_box == lax.broadcasted_iota(jnp.int32, (8, B * M), 0)
    loads[0].wait()

    def widen(src, dst):
        wide = src[...].astype(F32)
        for r in range(R):
            dst[pl.ds(2 * r, 2), :] = wide[r]

    widen(cur, cur32.at[1])
    for r in range(R):
        two = []
        for p in range(2):
            one = jnp.broadcast_to(cur32[1, pl.ds(2 * r + p, 1), :], (8, B * M))
            two.append(jnp.where(own_box, one, 0.0))
        expanded[pl.ds(16 * r, 16), :] = jnp.concatenate(two, axis=0).astype(BF16)

    loads[1].wait()

    def store_pairs(dst, real, imag):
        both = jnp.concatenate([real[:, None], imag[:, None]], axis=1)
        dst[...] = both.reshape(HROWS, S).astype(BF16)

    for h in range(H):
        rows = expanded[pl.ds(h * HROWS, HROWS), :]
        a = dot(rows, rad[0].reshape(B * M, S)).reshape(RH, 2, B, S)
        b = dot(rows, rad[1].reshape(B * M, S)).reshape(RH, 2, B, S)
        store_pairs(xb.at[0, h], a[:, 0] - b[:, 1], a[:, 1] + b[:, 0])

    far_peers = prev_far.astype(jnp.int32) + next_far.astype(jnp.int32)
    pl.semaphore_wait(barrier, NS - 1 + LINE - 1 + NY - 1 + far_peers)

    def level_copy(level, h):
        bit = 1 << level
        partner = samp + bit - 2 * bit * (samp // bit % 2)
        return remote(
            xb.at[level, h], yb.at[level, h], lev_ss.at[level, h], lev_rs.at[level, h], (box, partner)
        )

    for h in range(H):
        level_copy(0, h).start()

    to_next = remote(cur, halo.at[0], halo_ss.at[0], halo_rs.at[0], next_dev)
    to_prev = remote(cur, halo.at[1], halo_ss.at[1], halo_rs.at[1], prev_dev)

    @pl.when(has_next)
    def _():
        to_next.start()

    @pl.when(has_prev)
    def _():
        to_prev.start()

    def table_copy(k):
        to = (g + k) % LINE
        return remote(tb.at[to], tr.at[g], tab_ss.at[k], tab_rs.at[k], (line0 + to, samp))

    for k in range(1, LINE):
        table_copy(k).start()
    tr[g] = tb[g]

    @pl.when(has_prev)
    def _():
        to_next.wait_recv()

    @pl.when(jnp.logical_not(has_prev))
    def _():
        halo[0] = jnp.zeros((R, 2, B * M), BF16)

    @pl.when(has_next)
    def _():
        to_prev.wait_recv()

    @pl.when(jnp.logical_not(has_next))
    def _():
        halo[1] = jnp.zeros((R, 2, B * M), BF16)

    widen(halo.at[0], cur32.at[0])
    widen(halo.at[1], cur32.at[2])
    odd = lax.broadcasted_iota(jnp.int32, (2 * R, B * M), 0) % 2
    for part in range(3):
        plain = cur32[part]
        turned = jnp.where(
            odd == 1, pltpu.roll(plain, 1, 0), -pltpu.roll(plain, 2 * R - 1, 0)
        )
        for b in range(B):
            grid[0, part * B + b] = plain[:, b * M : (b + 1) * M].astype(BF16)
            grid[1, part * B + b] = turned[:, b * M : (b + 1) * M].astype(BF16)
    loads[3].wait()
    first = box * B - B

    def near_one(n, carry):
        source = jnp.clip(nidx_s[1, n] - first, 0, 3 * B - 1)
        near_y[n] = dot_nt(grid[0, source], nb[0, n]) + dot_nt(grid[1, source], nb[1, n])
        return carry

    lax.fori_loop(0, NEAR, near_one, 0, unroll=4)

    def near_add(n, carry):
        target = nidx_s[0, n] - first - B
        value = near_y[n]
        return tuple(
            total + value * jnp.where(target == d, 1.0, 0.0) for d, total in enumerate(carry)
        )

    sums = lax.fori_loop(
        0, NEAR, near_add, tuple(jnp.zeros((2 * R, M), F32) for _ in range(B)), unroll=2
    )
    for q in range(B // 2):
        near2d[q] = jnp.concatenate([sums[2 * q], sums[2 * q + 1]], axis=1)

    loads[2].wait()

    def level_step(level, h, dst):
        own = xb[level, h]
        pair = yb[level, h]
        a = (dot(own, itp[0, level, 0]) + dot(pair, itp[0, level, 1])).reshape(RH, 2, B, S)
        b = (dot(own, itp[1, level, 0]) + dot(pair, itp[1, level, 1])).reshape(RH, 2, B, S)
        store_pairs(dst, a[:, 0] - b[:, 1], a[:, 1] + b[:, 0])

    for h in range(H):
        level_copy(0, h).wait_recv()
        level_step(0, h, xb.at[1, h])
        level_copy(1, h).start()

    for k in range(1, LINE):
        table_copy(k).wait_recv()
    loads[4].wait()
    slots = tr[...]
    flat = slots.reshape(128, 128)
    type_lane = lax.broadcasted_iota(jnp.int32, (128, TYPES), 1)
    lane = lax.broadcasted_iota(jnp.int32, (LINE, 8, 128), 2)
    slot_y = lax.broadcasted_iota(jnp.int32, (LINE, 8, 128), 1) // 2
    hot = []
    for e in range(PER):
        pick = jnp.where(flat[:, 1 + e : 2 + e] == type_lane, 1.0, 0.0).astype(BF16)
        for p in range(2):
            ops[e, p] = dot(pick, trn[p]).reshape(LINE, 8, S)
        good = jnp.logical_and(slots[:, :, 3 + e : 4 + e] == lane % B, lane // B == slot_y)
        hot.append(jnp.where(good, 1.0, 0.0)[:, None])
    spread = jnp.concatenate(hot, axis=1).reshape(2 * 128, 128)
    hm[...] = jnp.transpose(spread)[: NY * B].astype(BF16)

    for h in range(H):
        level_copy(1, h).wait_recv()
        level_step(1, h, xb.at[2, h])
        level_copy(2, h).start()

    def piece(z, core, h):
        return xg.at[z * NC + core, pl.ds(h * HROWS, HROWS)]

    def to_right(z, h):
        return remote(piece(z, c, h), piece(z, c, h), right_ss.at[z, h], right_rs.at[z, h], zr_dev)

    def to_left(z, h):
        return remote(piece(z, c, h), piece(z, c, h), left_ss.at[z, h], left_rs.at[z, h], zl_dev)

    def to_sib(z, h):
        return remote(piece(z, c, h), piece(z, c, h), sib_ss.at[z, h], sib_rs.at[z, h], sib_dev)

    def from_sib(z, h):
        there = piece(z, 1 - c, h)
        return remote(there, there, sib_ss.at[z, h], sib_rs.at[z, h], sib_dev)

    def translate(slot, h):
        index = jnp.broadcast_to(jnp.maximum(tr[slot][:, 0:1], 0), (8, S))
        op = [[ops[e, p, slot] for p in range(2)] for e in range(PER)]
        at = pl.multiple_of(slot * 16, 16)
        for k in range(RH):
            r = h * RH + k
            both = xg[slot, pl.ds(r * 16, 16), :].astype(F32)
            re = jnp.take_along_axis(both[:8], index, axis=0)
            im = jnp.take_along_axis(both[8:], index, axis=0)
            real = [op[e][0] * re - op[e][1] * im for e in range(PER)]
            imag = [op[e][0] * im + op[e][1] * re for e in range(PER)]
            pb[r, 0, pl.ds(at, 16), :] = jnp.concatenate(real, axis=0).astype(BF16)
            pb[r, 1, pl.ds(at, 16), :] = jnp.concatenate(imag, axis=0).astype(BF16)

    for h in range(H):
        level_copy(2, h).wait_recv()
        level_step(2, h, piece(zl, c, h))

        @pl.when(zl < NZ - 1)
        def _():
            to_right(zl, h).start()

        @pl.when(zl > 0)
        def _():
            to_left(zl, h).start()

        to_sib(zl, h).start()

    def sib_slot(z, h):
        from_sib(z, h).wait_recv()
        translate(z * NC + 1 - c, h)

    def distance(d, carry):
        lower = zl - d
        upper = zl + d
        for h in range(H):

            @pl.when(lower >= 0)
            def _():
                to_right(lower, h).wait_recv()

                @pl.when(zl < NZ - 1)
                def _():
                    to_right(lower, h).start()

                to_sib(lower, h).start()

            @pl.when(upper < NZ)
            def _():
                to_left(upper, h).wait_recv()

                @pl.when(zl > 0)
                def _():
                    to_left(upper, h).start()

                to_sib(upper, h).start()

            @pl.when(lower + 1 >= 0)
            def _():
                translate((lower + 1) * NC + c, h)
                sib_slot(lower + 1, h)

            @pl.when(jnp.logical_and(d > 1, upper - 1 < NZ))
            def _():
                translate((upper - 1) * NC + c, h)
                sib_slot(upper - 1, h)

        return carry

    lax.fori_loop(1, NZ + 1, distance, 0)

    def y_copy(k, h):
        to = (y + k) % NY
        part = pl.ds(h * HROWS, HROWS)
        return remote(
            sb.at[to, part], yr.at[y, part], y_ss.at[k, h], y_rs.at[k, h], ((box + k * LINE) % (NY * LINE), samp)
        )

    def fin_copy(s):
        return remote(fs.at[s], fr.at[samp], fin_ss.at[s], fin_rs.at[samp], (box, s))

    weights = hm[...]
    for h in range(H):
        for k in range(RH):
            r = h * RH + k
            real = dot(weights, pb[r, 0])
            imag = dot(weights, pb[r, 1])
            for q in range(NY):
                both = jnp.concatenate([real[q * B : (q + 1) * B], imag[q * B : (q + 1) * B]], axis=0)
                sf[q, pl.ds(r * 16, 16), :] = both
                sb[q, pl.ds(r * 16, 16), :] = both.astype(BF16)
        for k in range(1, NY):
            y_copy(k, h).start()

    for h in range(H):
        part = pl.ds(h * HROWS, HROWS)
        incoming = sf[y, part, :]
        for k in range(1, NY):
            y_copy(NY - k, h).wait_recv()
            incoming = incoming + yr[(y + k) % NY, part, :].astype(F32)
        rounded = incoming.astype(BF16)
        a = dot_nt(rounded, rad[0].reshape(B * M, S)).reshape(RH, 2, B, B * M)
        b = dot_nt(rounded, rad[1].reshape(B * M, S)).reshape(RH, 2, B, B * M)
        far = [a[:, 0] + b[:, 1], a[:, 1] - b[:, 0]]
        for p in range(2):
            picked = jnp.sum(jnp.where(own_box[None], far[p], 0.0), axis=1) * FAR_SCALE
            near = [near2d[q, pl.ds(h * 2 * RH + p, RH, stride=2), :] for q in range(B // 2)]
            total = picked + jnp.concatenate(near, axis=1)
            for k in range(RH):
                r = h * RH + k
                fs[r // 2, pl.ds(r % 2 * 2 + p, 1), :] = total[k : k + 1]
        for s in range(h * NS // H, (h + 1) * NS // H):

            @pl.when(s != samp)
            def _():
                fin_copy(s).start()

    total = fs[samp]
    for k in range(1, NS):
        s = (samp + k) % NS
        there = remote(fs.at[s], fr.at[s], fin_ss.at[s], fin_rs.at[s], (box, s))
        there.wait_recv()
        total = total + fr[s]
    out_ref[0] = total[0:2]
    out_ref[1] = total[2:4]

    for level in range(3):
        for h in range(H):
            level_copy(level, h).wait_send()

    @pl.when(has_next)
    def _():
        to_next.wait_send()

    @pl.when(has_prev)
    def _():
        to_prev.wait_send()

    for k in range(1, LINE):
        table_copy(k).wait_send()
    for k in range(1, NY):
        for h in range(H):
            y_copy(k, h).wait_send()

    def drain(z, carry):
        for h in range(H):

            @pl.when(jnp.logical_and(z <= zl, zl < NZ - 1))
            def _():
                to_right(z, h).wait_send()

            @pl.when(jnp.logical_and(z >= zl, zl > 0))
            def _():
                to_left(z, h).wait_send()

            to_sib(z, h).wait_send()
        return carry

    lax.fori_loop(0, NZ, drain, 0)
    for k in range(1, NS):
        fin_copy((samp + k) % NS).wait_send()


def local(
    currents, radiation, interp, translation, inter_owner, inter_local, inter_type, near_blocks, near_index
):
    hbm = pl.BlockSpec(memory_space=pl.ANY)
    smem = pl.BlockSpec(memory_space=pltpu.SMEM)
    dma = pltpu.SemaphoreType.DMA
    vmem = pltpu.VMEM
    return pl.pallas_call(
        kernel,
        out_shape=jax.ShapeDtypeStruct((2, 2, B * M), F32),
        in_specs=[hbm] * 5 + [smem] * 4,
        out_specs=pl.BlockSpec(memory_space=pltpu.VMEM),
        scratch_shapes=[
            vmem((R, 2, B * M), BF16),
            vmem((2, R, 2, B * M), BF16),
            vmem((2, B, M, S), BF16),
            vmem((2, 3, 2, S, S), BF16),
            vmem((2, TYPES, S), BF16),
            vmem((2, NEAR, M, M), BF16),
            vmem((3, 2 * R, B * M), F32),
            vmem((ROWS, B * M), BF16),
            vmem((2, 3 * B, 2 * R, M), BF16),
            vmem((NEAR, 2 * R, M), F32),
            vmem((B // 2, 2 * R, 2 * M), F32),
            vmem((3, H, HROWS, S), BF16),
            vmem((3, H, HROWS, S), BF16),
            vmem((LINE, ROWS, S), BF16),
            vmem((LINE, 8, 128), jnp.int32),
            vmem((LINE, 8, 128), jnp.int32),
            vmem((PER, 2, LINE, 8, S), F32),
            vmem((R, 2, 2 * 128, S), BF16),
            vmem((NY * B, 2 * 128), BF16),
            vmem((NY, ROWS, S), BF16),
            vmem((NY, ROWS, S), F32),
            vmem((NY, ROWS, S), BF16),
            vmem((NS, 4, B * M), F32),
            vmem((NS, 4, B * M), F32),
            dma((5,)),
            dma((2,)),
            dma((2,)),
            dma((3, H)),
            dma((3, H)),
            dma((LINE,)),
            dma((LINE,)),
            dma((NZ, H)),
            dma((NZ, H)),
            dma((NZ, H)),
            dma((NZ, H)),
            dma((NZ, H)),
            dma((NZ, H)),
            dma((NY, H)),
            dma((NY, H)),
            dma((NS,)),
            dma((NS,)),
        ],
        compiler_params=pltpu.CompilerParams(
            collective_id=0, has_side_effects=True, vmem_limit_bytes=56 * 2**20
        ),
    )(
        currents,
        radiation,
        interp,
        translation,
        near_blocks,
        inter_owner.T,
        jnp.transpose(inter_local, (1, 2, 0)).reshape(OWN * PER, B),
        jnp.transpose(inter_type, (1, 2, 0)).reshape(OWN * PER, B),
        near_index.T,
    )


def solution(mesh):
    in_specs = (
        P(None, None, "box"),
        P(None, "box", None, "samp"),
        P(None, None, None, "samp", None),
        P(None, None, "samp"),
        P("box", None),
        P("box", None, None),
        P("box", None, None),
        P(None, ("box", "samp"), None, None),
        P(("box", "samp"), None),
    )
    return jax.shard_map(local, mesh=mesh, in_specs=in_specs, out_specs=P("samp", None, "box"), check_vma=False)
```

time: 450 us -> 93.1 us (0.21)
  waiting for transfers between devices: 329 us -> 0 us
  Pallas kernels: 0 us -> 89.4 us
  starting transfers between devices: 47.9 us -> 0 us
  local copies, waits for them, and re-layouts: 34 us -> 3.01 us
  matrix products: 19.3 us -> 0 us
  between operations: 14.6 us -> 0.01 us
    all_to_all x2 -> x0, waiting for transfers between devices: 174 us -> none  [the longest x1 174 us: local(): lax.all_to_all(outgoing, 'box', split_axis=0, concat_axis=0, tiled=True)]
    unnamed x2 -> x0, waiting for transfers between devices: 145 us -> none
    pallas_call x0 -> x1, Pallas kernels: none -> 89.4 us  [local(): pl.pallas_call(kernel, out_shape=jax.ShapeDtypeStruct((2, 2, B * M), F32)...]
    ppermute x5 -> x0, starting transfers between devices: 25.3 us -> none  [the longest x3 21.9 us: swapped(): return lax.ppermute(block, axis, route)]
    all_to_all x2 -> x0, starting transfers between devices: 22.5 us -> none  [the longest x1 13.5 us: local(): lax.all_to_all(outgoing, 'box', split_axis=0, concat_axis=0, tiled=True)]
    scatter x3 -> x0, local copies, waits for them, and re-layouts: 20.6 us -> none  [the longest x2 16.9 us: local(): outgoing = jnp.zeros((box_count, capacity, entry_count, 2, rhs_count, sam...]
    dot_general x38 -> x0, matrix products: 19.3 us -> none  [the longest x1 6.63 us: local(): jnp.einsum('scpd,scpxrk->xdrk', target_hot, arrived, preferred_element_ty...]
    ppermute x5 -> x0, waiting for transfers between devices: 10.8 us -> none  [the longest x3 9.07 us: swapped(): return lax.ppermute(block, axis, route)]
  transfers between devices with their start and end apart: 8 -> 0, of which waited for: 5 -> 0; matrix products, arithmetic and copies ran while one was open for 9% -> 0% of each run, Pallas kernels for 0% -> 0%
where the time goes in v1:
time: 93.1 us; the launch traced here: 92.4 us
  Pallas kernels  89.4 us (96%)
  local copies, waits for them, and re-layouts  3.01 us (3%)
    pallas_call x1, Pallas kernels, local(): pl.pallas_call(kernel, out_shape=jax.ShapeDtypeStruct((2, 2, B * M), F32)...  89.4 us
    unnamed x2, local copies, waits for them, and re-layouts  3.01 us

profile of v1, /device:TPU:6, one launch (start us, length us, event | category | flops | bytes accessed | tf_op | source)
XLA Modules:
  0.0 92.4 jit_solution(3470064755971844693)
XLA Ops:
  0.0 1.7 %copy.10.trn_h = bf16[2,316,256]{2,1,0:T(8,128)(2,1)} copy(bf16[2,316,256]{2,0,1:T(2,128)(2,1)} %param.12) | data formatting | bytes 647168 | tf_op args[3]
  1.7 89.4 %shard_map.91 = f32[2,2,512]{2,1,0:T(2,128)} custom-call(bf16[16,2,512]{2,1,0:T(2,128)(2,1)} %cur_h.1, bf16[2,8,64,256]{3,2,1,0:T(8,128)(2,1)} %rad_h.1, bf16[2,3,2,256,256]{4,3,2,1,0:T(8,128)(2,1)} %itp_h.1, bf16[2,316,256]{2,1,0:T(8,128)(2,1)} %copy.10.trn_h, bf16[2,32,64,64]{3,2,1,0:T(8,128)(2,1)} %near_h.1, s32[4,8]{1,0:T(4,128)} %bitcast.10, ...), custom_call_target="tpu_custom_call" | custom-call | tf_op jit(solution)/shard_map/pallas_call | solution.py:523
  91.1 1.3 %copy.12 = f32[2,2,512]{2,1,0:T(2,128)} copy(f32[2,2,512]{2,1,0:T(2,128)} %shard_map.91) | data formatting | bytes 16384

commit v2 on v1

--- a/solution.py
+++ b/solution.py
@@ -13,16 +13,20 @@
 OWN = 4
 PER = 2
 TYPES = 316
+TROWS = 640
 R = 16
 B = 8
 S = 256
 NEAR = 32
 NY, NZ, NC = 4, 8, 2
 NS = 8
-H = 2
+H = 4
 RH = R // H
 ROWS = R * 2 * B
 HROWS = ROWS // H
+Q = 4
+RQ = R // Q
+QROWS = ROWS // Q
 LINE = NZ * NC
 F32 = jnp.float32
 BF16 = jnp.bfloat16
@@ -54,16 +58,21 @@
     itp_h,
     trn_h,
     near_h,
+    owner_h,
+    local_h,
+    type_h,
+    nidx_h,
+    out_ref,
     owner_s,
     local_s,
     type_s,
     nidx_s,
-    out_ref,
     cur,
     halo,
     rad,
     itp,
     trn,
+    trn32,
     nb,
     cur32,
     expanded,
@@ -146,6 +155,14 @@
         pltpu.make_async_copy(near_h, nb, in_sem.at[3]),
         pltpu.make_async_copy(trn_h, trn, in_sem.at[4]),
     ]
+    lists = [
+        pltpu.make_async_copy(owner_h, owner_s, in_sem.at[5]),
+        pltpu.make_async_copy(local_h, local_s, in_sem.at[6]),
+        pltpu.make_async_copy(type_h, type_s, in_sem.at[7]),
+        pltpu.make_async_copy(nidx_h, nidx_s, in_sem.at[8]),
+    ]
+    for load in lists:
+        load.start()
     for load in loads:
         load.start()
 
@@ -153,6 +170,9 @@
     lane8 = lax.broadcasted_iota(jnp.int32, (8, 128), 1)
     row_slot = row % 2
     row_owner = ((row // 2 % NY) * NZ + row // 16) * NC + row // 8 % NC
+
+    for load in lists:
+        load.wait()
 
     def add_box(b, carry):
         value, count = carry
@@ -215,6 +235,17 @@
         b = dot(rows, rad[1].reshape(B * M, S)).reshape(RH, 2, B, S)
         store_pairs(xb.at[0, h], a[:, 0] - b[:, 1], a[:, 1] + b[:, 0])
 
+    loads[4].wait()
+
+    def split(k, carry):
+        four = trn[pl.ds(k * 4, 4)].astype(F32)
+        rows = jnp.concatenate([four[u] for u in range(4)], axis=0)
+        trn32[pl.ds(pl.multiple_of(k * 8, 8), 8), :] = rows
+        return carry
+
+    lax.fori_loop(0, TYPES // 4, split, 0)
+    trn32[pl.ds(2 * TYPES, TROWS - 2 * TYPES), :] = jnp.zeros((TROWS - 2 * TYPES, S), F32)
+
     far_peers = prev_far.astype(jnp.int32) + next_far.astype(jnp.int32)
     pl.semaphore_wait(barrier, NS - 1 + LINE - 1 + NY - 1 + far_peers)
 
@@ -313,17 +344,18 @@
 
     for k in range(1, LINE):
         table_copy(k).wait_recv()
-    loads[4].wait()
+    operators = trn32[...].astype(BF16)
     slots = tr[...]
     flat = slots.reshape(128, 128)
-    type_lane = lax.broadcasted_iota(jnp.int32, (128, TYPES), 1)
+    type_lane = lax.broadcasted_iota(jnp.int32, (128, TROWS), 1)
     lane = lax.broadcasted_iota(jnp.int32, (LINE, 8, 128), 2)
     slot_y = lax.broadcasted_iota(jnp.int32, (LINE, 8, 128), 1) // 2
     hot = []
     for e in range(PER):
-        pick = jnp.where(flat[:, 1 + e : 2 + e] == type_lane, 1.0, 0.0).astype(BF16)
+        kind = flat[:, 1 + e : 2 + e]
         for p in range(2):
-            ops[e, p] = dot(pick, trn[p]).reshape(LINE, 8, S)
+            pick = jnp.where(2 * kind + p == type_lane, 1.0, 0.0).astype(BF16)
+            ops[e, p] = dot(pick, operators).reshape(LINE, 8, S)
         good = jnp.logical_and(slots[:, :, 3 + e : 4 + e] == lane % B, lane // B == slot_y)
         hot.append(jnp.where(good, 1.0, 0.0)[:, None])
     spread = jnp.concatenate(hot, axis=1).reshape(2 * 128, 128)
@@ -334,28 +366,28 @@
         level_step(1, h, xb.at[2, h])
         level_copy(2, h).start()
 
-    def piece(z, core, h):
-        return xg.at[z * NC + core, pl.ds(h * HROWS, HROWS)]
-
-    def to_right(z, h):
-        return remote(piece(z, c, h), piece(z, c, h), right_ss.at[z, h], right_rs.at[z, h], zr_dev)
-
-    def to_left(z, h):
-        return remote(piece(z, c, h), piece(z, c, h), left_ss.at[z, h], left_rs.at[z, h], zl_dev)
-
-    def to_sib(z, h):
-        return remote(piece(z, c, h), piece(z, c, h), sib_ss.at[z, h], sib_rs.at[z, h], sib_dev)
-
-    def from_sib(z, h):
-        there = piece(z, 1 - c, h)
-        return remote(there, there, sib_ss.at[z, h], sib_rs.at[z, h], sib_dev)
-
-    def translate(slot, h):
+    def piece(z, core, q):
+        return xg.at[z * NC + core, pl.ds(q * QROWS, QROWS)]
+
+    def to_right(z, q):
+        return remote(piece(z, c, q), piece(z, c, q), right_ss.at[z, q], right_rs.at[z, q], zr_dev)
+
+    def to_left(z, q):
+        return remote(piece(z, c, q), piece(z, c, q), left_ss.at[z, q], left_rs.at[z, q], zl_dev)
+
+    def to_sib(z, q):
+        return remote(piece(z, c, q), piece(z, c, q), sib_ss.at[z, q], sib_rs.at[z, q], sib_dev)
+
+    def from_sib(z, q):
+        there = piece(z, 1 - c, q)
+        return remote(there, there, sib_ss.at[z, q], sib_rs.at[z, q], sib_dev)
+
+    def translate(slot, q):
         index = jnp.broadcast_to(jnp.maximum(tr[slot][:, 0:1], 0), (8, S))
         op = [[ops[e, p, slot] for p in range(2)] for e in range(PER)]
         at = pl.multiple_of(slot * 16, 16)
-        for k in range(RH):
-            r = h * RH + k
+        for k in range(RQ):
+            r = q * RQ + k
             both = xg[slot, pl.ds(r * 16, 16), :].astype(F32)
             re = jnp.take_along_axis(both[:8], index, axis=0)
             im = jnp.take_along_axis(both[8:], index, axis=0)
@@ -366,60 +398,65 @@
 
     for h in range(H):
         level_copy(2, h).wait_recv()
-        level_step(2, h, piece(zl, c, h))
-
-        @pl.when(zl < NZ - 1)
-        def _():
-            to_right(zl, h).start()
-
-        @pl.when(zl > 0)
-        def _():
-            to_left(zl, h).start()
-
-        to_sib(zl, h).start()
-
-    def sib_slot(z, h):
-        from_sib(z, h).wait_recv()
-        translate(z * NC + 1 - c, h)
-
-    def distance(d, carry):
+        level_step(2, h, xg.at[g, pl.ds(h * HROWS, HROWS)])
+
+        for q in range(h * Q // H, (h + 1) * Q // H):
+
+            @pl.when(zl < NZ - 1)
+            def _():
+                to_right(zl, q).start()
+
+            @pl.when(zl > 0)
+            def _():
+                to_left(zl, q).start()
+
+        for q in range(h * Q // H, (h + 1) * Q // H):
+            to_sib(zl, q).start()
+
+    def sib_slot(z, q):
+        from_sib(z, q).wait_recv()
+        translate(z * NC + 1 - c, q)
+
+    def step(d, q):
         lower = zl - d
         upper = zl + d
-        for h in range(H):
-
-            @pl.when(lower >= 0)
+
+        @pl.when(lower >= 0)
+        def _():
+            to_right(lower, q).wait_recv()
+
+            @pl.when(zl < NZ - 1)
             def _():
-                to_right(lower, h).wait_recv()
-
-                @pl.when(zl < NZ - 1)
-                def _():
-                    to_right(lower, h).start()
-
-                to_sib(lower, h).start()
-
-            @pl.when(upper < NZ)
+                to_right(lower, q).start()
+
+            to_sib(lower, q).start()
+
+        @pl.when(upper < NZ)
+        def _():
+            to_left(upper, q).wait_recv()
+
+            @pl.when(zl > 0)
             def _():
-                to_left(upper, h).wait_recv()
-
-                @pl.when(zl > 0)
-                def _():
-                    to_left(upper, h).start()
-
-                to_sib(upper, h).start()
-
-            @pl.when(lower + 1 >= 0)
-            def _():
-                translate((lower + 1) * NC + c, h)
-                sib_slot(lower + 1, h)
-
-            @pl.when(jnp.logical_and(d > 1, upper - 1 < NZ))
-            def _():
-                translate((upper - 1) * NC + c, h)
-                sib_slot(upper - 1, h)
-
+                to_left(upper, q).start()
+
+            to_sib(upper, q).start()
+
+        @pl.when(lower + 1 >= 0)
+        def _():
+            translate((lower + 1) * NC + c, q)
+            sib_slot(lower + 1, q)
+
+        @pl.when(jnp.logical_and(d > 1, upper - 1 < NZ))
+        def _():
+            translate((upper - 1) * NC + c, q)
+            sib_slot(upper - 1, q)
+
+    def distance(d, carry):
+        for q in range(Q):
+            step(d, q)
         return carry
 
-    lax.fori_loop(1, NZ + 1, distance, 0)
+    lax.fori_loop(1, NZ - 1, distance, 0)
 
     def y_copy(k, h):
         to = (y + k) % NY
@@ -433,6 +470,12 @@
 
     weights = hm[...]
     for h in range(H):
+
+        def last(d, carry):
+            step(d, h)
+            return carry
+
+        lax.fori_loop(NZ - 1, NZ + 1, last, 0)
         for k in range(RH):
             r = h * RH + k
             real = dot(weights, pb[r, 0])
@@ -473,8 +516,9 @@
         there = remote(fs.at[s], fr.at[s], fin_ss.at[s], fin_rs.at[s], (box, s))
         there.wait_recv()
         total = total + fr[s]
-    out_ref[0] = total[0:2]
-    out_ref[1] = total[2:4]
+    for r in range(2):
+        for q in range(B // 2):
+            out_ref[pl.ds(r * B + 2 * q, 2), :] = total[2 * r : 2 * r + 2, q * 2 * M : (q + 1) * 2 * M]
 
     for level in range(3):
         for h in range(H):
@@ -495,17 +539,17 @@
             y_copy(k, h).wait_send()
 
     def drain(z, carry):
-        for h in range(H):
+        for q in range(Q):
 
             @pl.when(jnp.logical_and(z <= zl, zl < NZ - 1))
             def _():
-                to_right(z, h).wait_send()
+                to_right(z, q).wait_send()
 
             @pl.when(jnp.logical_and(z >= zl, zl > 0))
             def _():
-                to_left(z, h).wait_send()
-
-            to_sib(z, h).wait_send()
+                to_left(z, q).wait_send()
+
+            to_sib(z, q).wait_send()
         return carry
 
     lax.fori_loop(0, NZ, drain, 0)
@@ -517,20 +561,25 @@
     currents, radiation, interp, translation, inter_owner, inter_local, inter_type, near_blocks, near_index
 ):
     hbm = pl.BlockSpec(memory_space=pl.ANY)
-    smem = pl.BlockSpec(memory_space=pltpu.SMEM)
+    smem = pltpu.SMEM
     dma = pltpu.SemaphoreType.DMA
     vmem = pltpu.VMEM
-    return pl.pallas_call(
+    rows = pl.pallas_call(
         kernel,
-        out_shape=jax.ShapeDtypeStruct((2, 2, B * M), F32),
-        in_specs=[hbm] * 5 + [smem] * 4,
+        out_shape=jax.ShapeDtypeStruct((2 * B, 2 * M), F32),
+        in_specs=[hbm] * 9,
         out_specs=pl.BlockSpec(memory_space=pltpu.VMEM),
         scratch_shapes=[
+            smem((OWN, B), jnp.int32),
+            smem((OWN * PER, B), jnp.int32),
+            smem((OWN * PER, B), jnp.int32),
+            smem((2, NEAR), jnp.int32),
             vmem((R, 2, B * M), BF16),
             vmem((2, R, 2, B * M), BF16),
             vmem((2, B, M, S), BF16),
             vmem((2, 3, 2, S, S), BF16),
-            vmem((2, TYPES, S), BF16),
+            vmem((TYPES, 2, S), BF16),
+            vmem((TROWS, S), F32),
             vmem((2, NEAR, M, M), BF16),
             vmem((3, 2 * R, B * M), F32),
             vmem((ROWS, B * M), BF16),
@@ -550,19 +599,19 @@
             vmem((NY, ROWS, S), BF16),
             vmem((NS, 4, B * M), F32),
             vmem((NS, 4, B * M), F32),
-            dma((5,)),
+            dma((9,)),
             dma((2,)),
             dma((2,)),
             dma((3, H)),
             dma((3, H)),
             dma((LINE,)),
             dma((LINE,)),
-            dma((NZ, H)),
-            dma((NZ, H)),
-            dma((NZ, H)),
-            dma((NZ, H)),
-            dma((NZ, H)),
-            dma((NZ, H)),
+            dma((NZ, Q)),
+            dma((NZ, Q)),
+            dma((NZ, Q)),
+            dma((NZ, Q)),
+            dma((NZ, Q)),
+            dma((NZ, Q)),
             dma((NY, H)),
             dma((NY, H)),
             dma((NS,)),
@@ -575,13 +624,14 @@
         currents,
         radiation,
         interp,
-        translation,
+        jnp.transpose(translation, (1, 0, 2)),
         near_blocks,
         inter_owner.T,
         jnp.transpose(inter_local, (1, 2, 0)).reshape(OWN * PER, B),
         jnp.transpose(inter_type, (1, 2, 0)).reshape(OWN * PER, B),
         near_index.T,
     )
+    return rows.reshape(2, B // 2, 2, 2 * M).transpose(0, 2, 1, 3).reshape(2, 2, B * M)
 
 
 def solution(mesh):

time: 93.1 us -> 85.5 us (0.918)
  Pallas kernels: 89.4 us -> 84 us
  local copies, waits for them, and re-layouts: 3.01 us -> 1.3 us
    pallas_call x1, Pallas kernels: 89.4 us -> 84 us  [local(): pl.pallas_call(kernel, out_shape=jax.ShapeDtypeStruct((2 * B, 2 * M), F32...]
    unnamed x2 -> x1, local copies, waits for them, and re-layouts: 3.01 us -> 1.3 us
where the time goes in v2:
time: 85.5 us; the launch traced here: 85.3 us
  Pallas kernels  84 us (98%)
  local copies, waits for them, and re-layouts  1.3 us (2%)
    pallas_call x1, Pallas kernels, local(): pl.pallas_call(kernel, out_shape=jax.ShapeDtypeStruct((2 * B, 2 * M), F32...  84 us

profile of v2, /device:TPU:6, one launch (start us, length us, event | category | flops | bytes accessed | tf_op | source)
XLA Modules:
  0.0 85.3 jit_solution(9600685737732035983)
XLA Ops:
  0.0 84.0 %shard_map.91 = f32[16,128]{1,0:T(8,128)} custom-call(bf16[16,2,512]{2,1,0:T(2,128)(2,1)} %cur_h.1, bf16[2,8,64,256]{3,2,1,0:T(8,128)(2,1)} %rad_h.1, bf16[2,3,2,256,256]{4,3,2,1,0:T(8,128)(2,1)} %itp_h.1, bf16[316,2,256]{2,1,0:T(2,128)(2,1)} %bitcast.14, bf16[2,32,64,64]{3,2,1,0:T(8,128)(2,1)} %near_h.1, s32[4,8]{1,0:T(4,128)} %bitcast.18, ...), custom_call_target="tpu_custom_call" | custom-call | tf_op jit(solution)/shard_map/pallas_call | solution.py:567
  84.0 1.3 %copy.12 = f32[2,2,512]{2,1,0:T(2,128)} copy(f32[2,2,512]{2,1,0:T(2,128)} %bitcast.15) | data formatting | bytes 16384

commit v3 on v2

--- a/solution.py
+++ b/solution.py
@@ -81,6 +81,8 @@
     near2d,
     xb,
     yb,
+    xm,
+    wp,
     xg,
     tb,
     tr,
@@ -97,6 +99,8 @@
     halo_rs,
     lev_ss,
     lev_rs,
+    wt_ss,
+    wt_rs,
     tab_ss,
     tab_rs,
     right_ss,
@@ -249,15 +253,27 @@
     far_peers = prev_far.astype(jnp.int32) + next_far.astype(jnp.int32)
     pl.semaphore_wait(barrier, NS - 1 + LINE - 1 + NY - 1 + far_peers)
 
-    def level_copy(level, h):
-        bit = 1 << level
-        partner = samp + bit - 2 * bit * (samp // bit % 2)
-        return remote(
-            xb.at[level, h], yb.at[level, h], lev_ss.at[level, h], lev_rs.at[level, h], (box, partner)
-        )
+    def flip(bits):
+        other = samp
+        for bit in (1, 2, 4):
+            if bits & bit:
+                other = other + bit - 2 * bit * (samp // bit % 2)
+        return (box, other)
+
+    def first_copy(h):
+        return remote(xb.at[0, h], yb.at[0, h], lev_ss.at[0, h], lev_rs.at[0, h], flip(1))
+
+    def second_copy(k, h):
+        return remote(xb.at[1, h], xm.at[k - 1, h], lev_ss.at[k, h], lev_rs.at[k, h], flip(2 * k))
+
+    def weight_copy(p):
+        return remote(itp.at[p, 1], wp.at[p], wt_ss.at[p], wt_rs.at[p], flip(4))
 
     for h in range(H):
-        level_copy(0, h).start()
+        first_copy(h).start()
+    loads[2].wait()
+    for p in range(2):
+        weight_copy(p).start()
 
     to_next = remote(cur, halo.at[0], halo_ss.at[0], halo_rs.at[0], next_dev)
     to_prev = remote(cur, halo.at[1], halo_ss.at[1], halo_rs.at[1], prev_dev)
@@ -277,6 +293,17 @@
     for k in range(1, LINE):
         table_copy(k).start()
     tr[g] = tb[g]
+
+    def level_step(own, pair, weight, dst):
+        a = (dot(own, weight(0, 0)) + dot(pair, weight(0, 1))).reshape(RH, 2, B, S)
+        b = (dot(own, weight(1, 0)) + dot(pair, weight(1, 1))).reshape(RH, 2, B, S)
+        store_pairs(dst, a[:, 0] - b[:, 1], a[:, 1] + b[:, 0])
+
+    for h in range(H):
+        first_copy(h).wait_recv()
+        level_step(xb[0, h], yb[0, h], lambda p, k: itp[p, 0, k], xb.at[1, h])
+        for k in (2, 3, 1):
+            second_copy(k, h).start()
 
     @pl.when(has_prev)
     def _():
@@ -308,39 +335,9 @@
     loads[3].wait()
     first = box * B - B
 
-    def near_one(n, carry):
+    def near_one(n):
         source = jnp.clip(nidx_s[1, n] - first, 0, 3 * B - 1)
         near_y[n] = dot_nt(grid[0, source], nb[0, n]) + dot_nt(grid[1, source], nb[1, n])
-        return carry
-
-    lax.fori_loop(0, NEAR, near_one, 0, unroll=4)
-
-    def near_add(n, carry):
-        target = nidx_s[0, n] - first - B
-        value = near_y[n]
-        return tuple(
-            total + value * jnp.where(target == d, 1.0, 0.0) for d, total in enumerate(carry)
-        )
-
-    sums = lax.fori_loop(
-        0, NEAR, near_add, tuple(jnp.zeros((2 * R, M), F32) for _ in range(B)), unroll=2
-    )
-    for q in range(B // 2):
-        near2d[q] = jnp.concatenate([sums[2 * q], sums[2 * q + 1]], axis=1)
-
-    loads[2].wait()
-
-    def level_step(level, h, dst):
-        own = xb[level, h]
-        pair = yb[level, h]
-        a = (dot(own, itp[0, level, 0]) + dot(pair, itp[0, level, 1])).reshape(RH, 2, B, S)
-        b = (dot(own, itp[1, level, 0]) + dot(pair, itp[1, level, 1])).reshape(RH, 2, B, S)
-        store_pairs(dst, a[:, 0] - b[:, 1], a[:, 1] + b[:, 0])
-
-    for h in range(H):
-        level_copy(0, h).wait_recv()
-        level_step(0, h, xb.at[1, h])
-        level_copy(1, h).start()
 
     for k in range(1, LINE):
         table_copy(k).wait_recv()
@@ -361,11 +358,6 @@
     spread = jnp.concatenate(hot, axis=1).reshape(2 * 128, 128)
     hm[...] = jnp.transpose(spread)[: NY * B].astype(BF16)
 
-    for h in range(H):
-        level_copy(1, h).wait_recv()
-        level_step(1, h, xb.at[2, h])
-        level_copy(2, h).start()
-
     def piece(z, core, q):
         return xg.at[z * NC + core, pl.ds(q * QROWS, QROWS)]
 
@@ -396,22 +388,22 @@
             pb[r, 0, pl.ds(at, 16), :] = jnp.concatenate(real, axis=0).astype(BF16)
             pb[r, 1, pl.ds(at, 16), :] = jnp.concatenate(imag, axis=0).astype(BF16)
 
-    for h in range(H):
-        level_copy(2, h).wait_recv()
-        level_step(2, h, xg.at[g, pl.ds(h * HROWS, HROWS)])
-
-        for q in range(h * Q // H, (h + 1) * Q // H):
-
-            @pl.when(zl < NZ - 1)
-            def _():
-                to_right(zl, q).start()
-
-            @pl.when(zl > 0)
-            def _():
-                to_left(zl, q).start()
-
-        for q in range(h * Q // H, (h + 1) * Q // H):
-            to_sib(zl, q).start()
+    def own_piece(q):
+        for k in range(1, 4):
+            second_copy(k, q).wait_recv()
+        level_step(xb[1, q], xm[0, q], lambda p, k: itp[p, 1, k], xb.at[2, q])
+        level_step(xm[1, q], xm[2, q], lambda p, k: wp[p, k], yb.at[1, q])
+        level_step(xb[2, q], yb[1, q], lambda p, k: itp[p, 2, k], xg.at[g, pl.ds(q * QROWS, QROWS)])
+
+        @pl.when(zl < NZ - 1)
+        def _():
+            to_right(zl, q).start()
+
+        @pl.when(zl > 0)
+        def _():
+            to_left(zl, q).start()
+
+        to_sib(zl, q).start()
 
     def sib_slot(z, q):
         from_sib(z, q).wait_recv()
@@ -451,12 +443,20 @@
             translate((upper - 1) * NC + c, q)
             sib_slot(upper - 1, q)
 
+    for p in range(2):
+        weight_copy(p).wait_recv()
+    for q in range(Q):
+        own_piece(q)
+
     def distance(d, carry):
         for q in range(Q):
             step(d, q)
+            near_one(4 * (d - 1) + q)
         return carry
 
     lax.fori_loop(1, NZ - 1, distance, 0)
+    for n in range(NEAR - 8, NEAR):
+        near_one(n)
 
     def y_copy(k, h):
         to = (y + k) % NY
@@ -469,13 +469,8 @@
         return remote(fs.at[s], fr.at[samp], fin_ss.at[s], fin_rs.at[samp], (box, s))
 
     weights = hm[...]
-    for h in range(H):
-
-        def last(d, carry):
-            step(d, h)
-            return carry
-
-        lax.fori_loop(NZ - 1, NZ + 1, last, 0)
+
+    def finish(h):
         for k in range(RH):
             r = h * RH + k
             real = dot(weights, pb[r, 0])
@@ -486,6 +481,24 @@
                 sb[q, pl.ds(r * 16, 16), :] = both.astype(BF16)
         for k in range(1, NY):
             y_copy(k, h).start()
+
+    for q in range(Q):
+        step(NZ - 1, q)
+        step(NZ, q)
+        finish(q)
+
+    def near_add(n, carry):
+        target = nidx_s[0, n] - first - B
+        value = near_y[n]
+        return tuple(
+            total + value * jnp.where(target == d, 1.0, 0.0) for d, total in enumerate(carry)
+        )
+
+    sums = lax.fori_loop(
+        0, NEAR, near_add, tuple(jnp.zeros((2 * R, M), F32) for _ in range(B)), unroll=2
+    )
+    for q in range(B // 2):
+        near2d[q] = jnp.concatenate([sums[2 * q], sums[2 * q + 1]], axis=1)
 
     for h in range(H):
         part = pl.ds(h * HROWS, HROWS)
@@ -510,19 +523,25 @@
             def _():
                 fin_copy(s).start()
 
-    total = fs[samp]
+    own = fs[samp]
+    others = jnp.zeros((4, B * M), F32)
     for k in range(1, NS):
         s = (samp + k) % NS
         there = remote(fs.at[s], fr.at[s], fin_ss.at[s], fin_rs.at[s], (box, s))
         there.wait_recv()
-        total = total + fr[s]
-    for r in range(2):
-        for q in range(B // 2):
-            out_ref[pl.ds(r * B + 2 * q, 2), :] = total[2 * r : 2 * r + 2, q * 2 * M : (q + 1) * 2 * M]
-
-    for level in range(3):
-        for h in range(H):
-            level_copy(level, h).wait_send()
+        others = others + fr[s]
+    for half, total in enumerate((own, others)):
+        for r in range(2):
+            for q in range(B // 2):
+                at = pl.ds(r * B + 2 * q, 2)
+                out_ref[half, at, :] = total[2 * r : 2 * r + 2, q * 2 * M : (q + 1) * 2 * M]
+
+    for h in range(H):
+        first_copy(h).wait_send()
+        for k in range(1, 4):
+            second_copy(k, h).wait_send()
+    for p in range(2):
+        weight_copy(p).wait_send()
 
     @pl.when(has_next)
     def _():
@@ -566,7 +585,7 @@
     vmem = pltpu.VMEM
     rows = pl.pallas_call(
         kernel,
-        out_shape=jax.ShapeDtypeStruct((2 * B, 2 * M), F32),
+        out_shape=jax.ShapeDtypeStruct((2, 2 * B, 2 * M), F32),
         in_specs=[hbm] * 9,
         out_specs=pl.BlockSpec(memory_space=pltpu.VMEM),
         scratch_shapes=[
@@ -587,7 +606,9 @@
             vmem((NEAR, 2 * R, M), F32),
             vmem((B // 2, 2 * R, 2 * M), F32),
             vmem((3, H, HROWS, S), BF16),
+            vmem((2, H, HROWS, S), BF16),
             vmem((3, H, HROWS, S), BF16),
+            vmem((2, 2, S, S), BF16),
             vmem((LINE, ROWS, S), BF16),
             vmem((LINE, 8, 128), jnp.int32),
             vmem((LINE, 8, 128), jnp.int32),
@@ -602,8 +623,10 @@
             dma((9,)),
             dma((2,)),
             dma((2,)),
-            dma((3, H)),
-            dma((3, H)),
+            dma((4, H)),
+            dma((4, H)),
+            dma((2,)),
+            dma((2,)),
             dma((LINE,)),
             dma((LINE,)),
             dma((NZ, Q)),
@@ -631,7 +654,7 @@
         jnp.transpose(inter_type, (1, 2, 0)).reshape(OWN * PER, B),
         near_index.T,
     )
-    return rows.reshape(2, B // 2, 2, 2 * M).transpose(0, 2, 1, 3).reshape(2, 2, B * M)
+    return (rows[0] + rows[1]).reshape(2, B // 2, 2, 2 * M).transpose(0, 2, 1, 3).reshape(2, 2, B * M)
 
 
 def solution(mesh):

time: 85.5 us -> 83.5 us (0.977)
  Pallas kernels: 84 us -> 82 us
  other arithmetic: 0 us -> 1.32 us
  local copies, waits for them, and re-layouts: 1.3 us -> 0 us
    pallas_call x1, Pallas kernels: 84 us -> 82 us  [local(): pl.pallas_call(kernel, out_shape=jax.ShapeDtypeStruct((2, 2 * B, 2 * M),...]
    add x0 -> x1, other arithmetic: none -> 1.32 us  [local(): rows[0] + rows[1]]
    unnamed x1 -> x0, local copies, waits for them, and re-layouts: 1.3 us -> none
where the time goes in v3:
time: 83.5 us; the launch traced here: 83.3 us
  Pallas kernels  82 us (98%)
  other arithmetic  1.32 us (2%)
    pallas_call x1, Pallas kernels, local(): pl.pallas_call(kernel, out_shape=jax.ShapeDtypeStruct((2, 2 * B, 2 * M),...  82 us

profile of v3, /device:TPU:6, one launch (start us, length us, event | category | flops | bytes accessed | tf_op | source)
XLA Modules:
  0.0 83.3 jit_solution(15557187007868121790)
XLA Ops:
  0.0 82.0 %shard_map.91 = f32[2,16,128]{2,1,0:T(8,128)} custom-call(bf16[16,2,512]{2,1,0:T(2,128)(2,1)} %cur_h.1, bf16[2,8,64,256]{3,2,1,0:T(8,128)(2,1)} %rad_h.1, bf16[2,3,2,256,256]{4,3,2,1,0:T(8,128)(2,1)} %itp_h.1, bf16[316,2,256]{2,1,0:T(2,128)(2,1)} %bitcast.14, bf16[2,32,64,64]{3,2,1,0:T(8,128)(2,1)} %near_h.1, s32[4,8]{1,0:T(4,128)} %bitcast.17, ...), custom_call_target="tpu_custom_call" | custom-call | tf_op jit(solution)/shard_map/pallas_call | solution.py:586
  82.0 1.3 %slice_add_fusion = f32[1,16,128]{2,1,0:T(8,128)} fusion(f32[2,16,128]{2,1,0:T(8,128)} %shard_map.91), kind=kLoop, calls=%fused_computation | loop fusion | flops 2048 | bytes 24576 | tf_op jit(solution)/shard_map/add | solution.py:657

commit v4 on v3

--- a/solution.py
+++ b/solution.py
@@ -523,6 +523,42 @@
             def _():
                 fin_copy(s).start()
 
+    for h in range(H):
+        first_copy(h).wait_send()
+        for k in range(1, 4):
+            second_copy(k, h).wait_send()
+    for p in range(2):
+        weight_copy(p).wait_send()
+
+    @pl.when(has_next)
+    def _():
+        to_next.wait_send()
+
+    @pl.when(has_prev)
+    def _():
+        to_prev.wait_send()
+
+    for k in range(1, LINE):
+        table_copy(k).wait_send()
+    for k in range(1, NY):
+        for h in range(H):
+            y_copy(k, h).wait_send()
+
+    def drain(z, carry):
+        for q in range(Q):
+
+            @pl.when(jnp.logical_and(z <= zl, zl < NZ - 1))
+            def _():
+                to_right(z, q).wait_send()
+
+            @pl.when(jnp.logical_and(z >= zl, zl > 0))
+            def _():
+                to_left(z, q).wait_send()
+
+            to_sib(z, q).wait_send()
+        return carry
+
+    lax.fori_loop(0, NZ, drain, 0)
     own = fs[samp]
     others = jnp.zeros((4, B * M), F32)
     for k in range(1, NS):
@@ -536,42 +572,6 @@
                 at = pl.ds(r * B + 2 * q, 2)
                 out_ref[half, at, :] = total[2 * r : 2 * r + 2, q * 2 * M : (q + 1) * 2 * M]
 
-    for h in range(H):
-        first_copy(h).wait_send()
-        for k in range(1, 4):
-            second_copy(k, h).wait_send()
-    for p in range(2):
-        weight_copy(p).wait_send()
-
-    @pl.when(has_next)
-    def _():
-        to_next.wait_send()
-
-    @pl.when(has_prev)
-    def _():
-        to_prev.wait_send()
-
-    for k in range(1, LINE):
-        table_copy(k).wait_send()
-    for k in range(1, NY):
-        for h in range(H):
-            y_copy(k, h).wait_send()
-
-    def drain(z, carry):
-        for q in range(Q):
-
-            @pl.when(jnp.logical_and(z <= zl, zl < NZ - 1))
-            def _():
-                to_right(z, q).wait_send()
-
-            @pl.when(jnp.logical_and(z >= zl, zl > 0))
-            def _():
-                to_left(z, q).wait_send()
-
-            to_sib(z, q).wait_send()
-        return carry
-
-    lax.fori_loop(0, NZ, drain, 0)
     for k in range(1, NS):
         fin_copy((samp + k) % NS).wait_send()
 

time: 83.5 us -> 83.2 us (level)
  no operation moved by 1% of the time
where the time goes in v4:
time: 83.2 us; the launch traced here: 83.1 us
  Pallas kernels  81.7 us (98%)
  other arithmetic  1.32 us (2%)
    pallas_call x1, Pallas kernels, local(): pl.pallas_call(kernel, out_shape=jax.ShapeDtypeStruct((2, 2 * B, 2 * M),...  81.7 us

profile of v4, /device:TPU:6, one launch (start us, length us, event | category | flops | bytes accessed | tf_op | source)
XLA Modules:
  0.0 83.1 jit_solution(10250602137869460577)
XLA Ops:
  0.0 81.7 %shard_map.91 = f32[2,16,128]{2,1,0:T(8,128)} custom-call(bf16[16,2,512]{2,1,0:T(2,128)(2,1)} %cur_h.1, bf16[2,8,64,256]{3,2,1,0:T(8,128)(2,1)} %rad_h.1, bf16[2,3,2,256,256]{4,3,2,1,0:T(8,128)(2,1)} %itp_h.1, bf16[316,2,256]{2,1,0:T(2,128)(2,1)} %bitcast.14, bf16[2,32,64,64]{3,2,1,0:T(8,128)(2,1)} %near_h.1, s32[4,8]{1,0:T(4,128)} %bitcast.17, ...), custom_call_target="tpu_custom_call" | custom-call | tf_op jit(solution)/shard_map/pallas_call | solution.py:586
  81.7 1.3 %slice_add_fusion = f32[1,16,128]{2,1,0:T(8,128)} fusion(f32[2,16,128]{2,1,0:T(8,128)} %shard_map.91), kind=kLoop, calls=%fused_computation | loop fusion | flops 2048 | bytes 24576 | tf_op jit(solution)/shard_map/add | solution.py:657

commit v5 on v4

--- a/solution.py
+++ b/solution.py
@@ -93,6 +93,7 @@
     sf,
     yr,
     fs,
+    fb,
     fr,
     in_sem,
     halo_ss,
@@ -465,8 +466,14 @@
             sb.at[to, part], yr.at[y, part], y_ss.at[k, h], y_rs.at[k, h], ((box + k * LINE) % (NY * LINE), samp)
         )
 
+    def in_rows(total):
+        cuts = [
+            total[2 * r : 2 * r + 2, q * 2 * M : (q + 1) * 2 * M] for r in range(2) for q in range(B // 2)
+        ]
+        return jnp.concatenate(cuts, axis=0)
+
     def fin_copy(s):
-        return remote(fs.at[s], fr.at[samp], fin_ss.at[s], fin_rs.at[samp], (box, s))
+        return remote(fb.at[s], fr.at[samp], fin_ss.at[s], fin_rs.at[samp], (box, s))
 
     weights = hm[...]
 
@@ -518,6 +525,7 @@
                 r = h * RH + k
                 fs[r // 2, pl.ds(r % 2 * 2 + p, 1), :] = total[k : k + 1]
         for s in range(h * NS // H, (h + 1) * NS // H):
+            fb[s] = in_rows(fs[s]).astype(BF16)
 
             @pl.when(s != samp)
             def _():
@@ -560,17 +568,14 @@
 
     lax.fori_loop(0, NZ, drain, 0)
     own = fs[samp]
-    others = jnp.zeros((4, B * M), F32)
+    others = jnp.zeros((2 * B, 2 * M), F32)
     for k in range(1, NS):
         s = (samp + k) % NS
-        there = remote(fs.at[s], fr.at[s], fin_ss.at[s], fin_rs.at[s], (box, s))
+        there = remote(fb.at[s], fr.at[s], fin_ss.at[s], fin_rs.at[s], (box, s))
         there.wait_recv()
-        others = others + fr[s]
-    for half, total in enumerate((own, others)):
-        for r in range(2):
-            for q in range(B // 2):
-                at = pl.ds(r * B + 2 * q, 2)
-                out_ref[half, at, :] = total[2 * r : 2 * r + 2, q * 2 * M : (q + 1) * 2 * M]
+        others = others + fr[s].astype(F32)
+    out_ref[0] = in_rows(own)
+    out_ref[1] = others
 
     for k in range(1, NS):
         fin_copy((samp + k) % NS).wait_send()
@@ -619,7 +624,8 @@
             vmem((NY, ROWS, S), F32),
             vmem((NY, ROWS, S), BF16),
             vmem((NS, 4, B * M), F32),
-            vmem((NS, 4, B * M), F32),
+            vmem((NS, 2 * B, 2 * M), BF16),
+            vmem((NS, 2 * B, 2 * M), BF16),
             dma((9,)),
             dma((2,)),
             dma((2,)),

time: 83.2 us -> 83.2 us (level)
  no operation moved by 1% of the time
where the time goes in v5:
time: 83.2 us; the launch traced here: 83 us
  Pallas kernels  81.7 us (98%)
  other arithmetic  1.32 us (2%)
    pallas_call x1, Pallas kernels, local(): pl.pallas_call(kernel, out_shape=jax.ShapeDtypeStruct((2, 2 * B, 2 * M),...  81.7 us

profile of v5, /device:TPU:6, one launch (start us, length us, event | category | flops | bytes accessed | tf_op | source)
XLA Modules:
  0.0 83.0 jit_solution(11320025177713706649)
XLA Ops:
  0.0 81.7 %shard_map.91 = f32[2,16,128]{2,1,0:T(8,128)} custom-call(bf16[16,2,512]{2,1,0:T(2,128)(2,1)} %cur_h.1, bf16[2,8,64,256]{3,2,1,0:T(8,128)(2,1)} %rad_h.1, bf16[2,3,2,256,256]{4,3,2,1,0:T(8,128)(2,1)} %itp_h.1, bf16[316,2,256]{2,1,0:T(2,128)(2,1)} %bitcast.14, bf16[2,32,64,64]{3,2,1,0:T(8,128)(2,1)} %near_h.1, s32[4,8]{1,0:T(4,128)} %bitcast.17, ...), custom_call_target="tpu_custom_call" | custom-call | tf_op jit(solution)/shard_map/pallas_call | solution.py:591
  81.7 1.3 %slice_add_fusion = f32[1,16,128]{2,1,0:T(8,128)} fusion(f32[2,16,128]{2,1,0:T(8,128)} %shard_map.91), kind=kLoop, calls=%fused_computation | loop fusion | flops 2048 | bytes 24576 | tf_op jit(solution)/shard_map/add | solution.py:663
